TPU v7x, 32 devices: a whole 2x2x4 slice. The times are simulated.
32 devices in a mesh: tm: 4 (over y, x), feed: 8 (over z, core).
Axes of the slice: x: 2, y: 2, z: 4, core: 2. Of those that a mesh axis runs over, the one named last changes fastest.
Arguments:
- voltages: int32 [2048, 32768], P('feed', 'tm'), may hold values from -128 to 127
- feed_at_grid_slot: int32 [2048], replicated, may hold values from 0 to 2047, each once
- ew_grid: int32 [4], replicated, may hold values from 0 to 511
- ns_grid: int32 [256], replicated, may hold values from 0 to 511
- delays: int32 [1024, 512], replicated, may hold values from 0 to 15, as said below
Outputs:
- dedispersed: float32 [512, 1024, 16], P('tm', 'feed')
Inputs may be any that keep to these rules, and one draw needn't show every extreme that they name: `feed_at_grid_slot`: each feed stands at exactly one grid position. delays are taken modulo 16.
All inputs are finite; a program needn't handle non-finite values.
Results may differ from a plain program's by a relative error of at most 0.017.
Values may be sent and summed in bfloat16 or wider, within the bound.
A program may use at most 128 MiB of HBM per device.

v0:
```python
from functools import partial
import math

import jax
import jax.numpy as jnp
from jax import lax
from jax.sharding import PartitionSpec as P

NFFT = 2048
CHANS = 1024
TAPS = 4
ROWS = 256


TWO_PI = 2.0 * math.pi
phase_modulus = 1048576


def from_behind(block, axis, distance):
    devices = range(lax.axis_size(axis))
    route = [(i - distance, i) for i in devices if i - distance in devices]
    return lax.ppermute(block, axis, route)


def pfb_window(tap_count, series_length):
    points = jnp.arange(tap_count * series_length, dtype=jnp.float32) + 0.5
    start_offset = points / series_length - tap_count / 2.0
    taper = 0.5 - 0.5 * jnp.cos(TWO_PI * points / (tap_count * series_length))
    values = (jnp.sinc(start_offset) * taper).reshape(tap_count, series_length)
    return values / jnp.sqrt(jnp.sum(values * values, axis=0, keepdims=True))


def dft_table(series_length, columns):
    product = (
        jnp.arange(series_length, dtype=jnp.int32)[:, None]
        * jnp.arange(columns, dtype=jnp.int32)[None, :]
        % series_length
    )
    angles = product.astype(jnp.float32) * (TWO_PI / series_length)
    factor = 1.0 / math.sqrt(series_length)
    return jnp.concatenate([jnp.cos(angles) * factor, -jnp.sin(angles) * factor], axis=1).astype(
        jnp.bfloat16
    )


def spectral_table(series_length):
    product = (
        jnp.arange(series_length, dtype=jnp.int32)[:, None]
        * jnp.arange(series_length, dtype=jnp.int32)[None, :]
        % series_length
    )
    angles = product.astype(jnp.float32) * (TWO_PI / series_length)
    factor = 1.0 / math.sqrt(series_length)
    nonzero = (jnp.arange(series_length) > 0)[:, None]
    cosine = jnp.where(nonzero, jnp.cos(angles) * factor, 0.0)
    sine_part = jnp.where(nonzero, -jnp.sin(angles) * factor, 0.0)
    return jnp.stack([cosine, sine_part]).astype(jnp.bfloat16)


def steer_table(coords, grid_ids, chan_ids, factor):
    phases = (
        coords[None, None, :] * grid_ids[None, :, None] * chan_ids[:, None, None] % phase_modulus
    )
    angles = phases.astype(jnp.float32) * (TWO_PI / phase_modulus)
    return (
        (jnp.cos(angles) * factor).astype(jnp.bfloat16),
        (jnp.sin(angles) * factor).astype(jnp.bfloat16),
    )


def form_beams(block_in, feed_at_grid_slot, ew_tables, ns_tables):
    ew_real, ew_imag = ew_tables
    ns_real, ns_imag = ns_tables
    item_count = block_in.shape[1]
    chan_count = block_in.shape[3]
    gridded = jnp.take(block_in, feed_at_grid_slot, axis=0).reshape(
        ROWS, 4, 2, item_count, 2, chan_count
    )
    grid_real = gridded[:, :, :, :, 0, :]
    grid_imag = gridded[:, :, :, :, 1, :]
    east_mix = partial(jnp.einsum, "cey,rypsc->erpsc", preferred_element_type=jnp.float32)
    east_real = (east_mix(ew_real, grid_real) - east_mix(ew_imag, grid_imag)).astype(jnp.bfloat16)
    east_imag = (east_mix(ew_real, grid_imag) + east_mix(ew_imag, grid_real)).astype(jnp.bfloat16)
    north_mix = partial(jnp.einsum, "cbr,erpsc->ebpsc", preferred_element_type=jnp.float32)
    beam_real = north_mix(ns_real, east_real) - north_mix(ns_imag, east_imag)
    beam_imag = north_mix(ns_real, east_imag) + north_mix(ns_imag, east_real)
    beam_power = jnp.sum(beam_real * beam_real + beam_imag * beam_imag, axis=2)
    return beam_power.reshape(-1, item_count, chan_count).astype(jnp.bfloat16)


def local(voltages, feed_at_grid_slot, ew_grid, ns_grid, delays):
    feed_dev = voltages.shape[0]
    spec_dev = voltages.shape[1] // NFFT
    time_extent = lax.axis_size("tm")
    feed_size = lax.axis_size("feed")
    spec_total = spec_dev * time_extent
    frames = (
        (voltages.astype(jnp.float32) / 64.0).astype(jnp.bfloat16).reshape(feed_dev, spec_dev, NFFT)
    )
    history = from_behind(frames[:, spec_dev - TAPS + 1 :, :], "tm", 1)
    padded = jnp.concatenate([history, frames], axis=1)
    window = pfb_window(TAPS, NFFT)
    filtered = jnp.zeros((feed_dev, spec_dev, NFFT), jnp.float32)
    for tap_index in range(TAPS):
        filtered = filtered + window[tap_index] * padded[
            :, tap_index : tap_index + spec_dev, :
        ].astype(jnp.float32)
    spectra = jnp.dot(
        filtered.astype(jnp.bfloat16).reshape(feed_dev * spec_dev, NFFT),
        dft_table(NFFT, CHANS),
        preferred_element_type=jnp.float32,
    )
    spectra = spectra.astype(jnp.bfloat16).reshape(feed_dev, spec_dev, 2, CHANS)
    chan_dev = CHANS // feed_size
    chan_ids = lax.axis_index("feed") * chan_dev + jnp.arange(chan_dev, dtype=jnp.int32) + CHANS
    ew_tables = steer_table(jnp.arange(4, dtype=jnp.int32), ew_grid, chan_ids, 0.5)
    ns_tables = steer_table(
        jnp.arange(ROWS, dtype=jnp.int32), ns_grid, chan_ids, 1.0 / math.sqrt(ROWS)
    )
    intensity = form_beams(
        lax.all_to_all(spectra, "feed", split_axis=3, concat_axis=0, tiled=True),
        feed_at_grid_slot,
        ew_tables,
        ns_tables,
    )
    time_table = spectral_table(spec_total)
    first_freq = lax.axis_index("tm") * spec_dev
    by_beam = lax.all_to_all(intensity, "feed", split_axis=0, concat_axis=2, tiled=True)
    my_table = lax.dynamic_slice_in_dim(time_table, first_freq, spec_dev, 1)
    zero_init = jnp.zeros((by_beam.shape[0], 2, spec_dev, CHANS), jnp.float32)
    spectrum = (
        zero_init
        + jnp.einsum(
            "rkt,btc->brkc",
            my_table,
            lax.all_gather(by_beam, "tm", axis=1, tiled=True),
            preferred_element_type=jnp.float32,
        )
    ).astype(jnp.bfloat16)
    freq_ids = first_freq + jnp.arange(spec_dev, dtype=jnp.int32)
    phases = freq_ids[:, None, None] * delays[None, :, :] % spec_total
    angles = phases.astype(jnp.float32) * (TWO_PI / spec_total)
    phase_real = jnp.cos(angles).astype(jnp.bfloat16)
    phase_imag = jnp.sin(angles).astype(jnp.bfloat16)
    shift_mixture = partial(jnp.einsum, "vuw,uwt->vut", preferred_element_type=jnp.float32)
    spec_real = spectrum[:, 0]
    spec_imag = spectrum[:, 1]
    moved_real = shift_mixture(spec_real, phase_real) - shift_mixture(spec_imag, phase_imag)
    moved_imag = shift_mixture(spec_real, phase_imag) + shift_mixture(spec_imag, phase_real)
    folded = (jnp.stack([moved_real, moved_imag], axis=1) * (1.0 / math.sqrt(CHANS))).astype(
        jnp.bfloat16
    )
    combined = lax.all_to_all(folded, "tm", split_axis=3, concat_axis=2, tiled=True)
    return jnp.einsum("brkd,rkt->dbt", combined, time_table, preferred_element_type=jnp.float32)


def solution(mesh):
    in_specs = (P("feed", "tm"), P(), P(), P(), P())
    out_specs = P("tm", "feed", None)
    return jax.shard_map(local, mesh=mesh, in_specs=in_specs, out_specs=out_specs, check_vma=False)
```

profile of v0, /device:TPU:0, one launch (start us, length us, event | category | flops | bytes accessed | tf_op | source)
XLA Modules:
  0.0 1157.7 jit_solution(12672029757183060693)
XLA Ops:
  6.5 9.0 copy.108
  32.1 35.2 %multiply_convert_fusion.2 = (bf16[2048,1024]{1,0:T(8,128)(2,1)}, bf16[2048,1024]{1,0:T(8,128)(2,1)}) fusion(), kind=kLoop, calls=%fused_computation.38 | loop fusion | flops 39845888 | bytes 8388608 | tf_op jit(solution)/shard_map/convert.1
  67.4 30.0 %collective-permute-done = bf16[256,3,2048]{2,0,1:T(8,128)(2,1)} collective-permute-done((bf16[256,3,2048]{2,0,1:T(8,128)(2,1)}, bf16[256,3,2048]{2,0,1:T(8,128)(2,1)}, u32[]{:S(2)}, u32[]{:S(2)}) %collective-permute-start) | collective-permute-done | bytes 3145760 | tf_op jit(solution)/shard_map/ppermute | solution.py:22
  100.6 8.2 add_convert_fusion
  108.7 7.9 copy.111
  116.6 6.9 reshape.210
  123.5 14.4 %fusion.30 = bf16[1024,2048]{1,0:T(8,128)(2,1)} fusion(bf16[1024,2048]{1,0:T(8,128)(2,1)} %reshape.210, bf16[2048,1024]{1,0:T(8,128)(2,1)} %get-tuple-element.13, bf16[2048,1024]{1,0:T(8,128)(2,1)} %get-tuple-element.14), kind=kOutput, calls=%fused_computation.57 | convolution fusion | flops 8608808960 | bytes 16777216 | tf_op jit(solution)/shard_map/dot_general | solution.py:108
  137.9 7.8 reshape.211
  145.7 16.2 %copy.112 = bf16[256,4,2,1024]{0,2,1,3:T(2,128)(2,1)} copy(bf16[256,4,2,1024]{3,2,1,0:T(2,128)(2,1)} %reshape.211) | data formatting | bytes 8388608 | tf_op jit(solution)/shard_map/reshape | solution.py:113
  168.0 92.8 %all-to-all-done = bf16[256,4,2,1024]{0,2,1,3:T(2,128)(2,1)} async-done(((bf16[256,4,2,1024]{0,2,1,3:T(2,128)(2,1)}), bf16[256,4,2,1024]{0,2,1,3:T(2,128)(2,1)}, u32[]{:S(2)}, u32[]{:S(2)}) %all-to-all-start) | async-done | bytes 4194336 | tf_op jit(solution)/shard_map/all_to_all | solution.py:121
  272.1 7.6 copy.115
  279.7 18.8 %gather_fusion = bf16[2048,4,2,128]{3,1,2,0:T(4,128)(2,1)} fusion(bf16[2048,4,2,128]{3,1,2,0:T(4,128)(2,1)} %copy.115, s32[2048]{0:T(1024)S(1)} %fusion.86), kind=kCustom, calls=%fused_computation | custom fusion | bytes 8396800 | tf_op jit(solution)/shard_map/jit(_take)/gather | solution.py:76
  298.4 9.0 copy.117
  320.7 136.5 %fusion.7 = f32[128,4,2,4,256]{4,3,2,1,0:T(4,128)S(1)} fusion(s32[128]{0:T(128)S(1)} %add_add_fusion, s32[256,256]{1,0:T(8,128)S(1)} %iota_multiply_fusion, bf16[4,256,2,4,128]{1,0,3,2,4:T(4,128)(2,1)S(1)} %fusion.43), kind=kOutput, calls=%fused_computation.14 | convolution fusion | flops 671088640 | bytes 6554112 | tf_op jit(solution)/shard_map/cbr,erpsc->ebpsc/dot_general | solution.py:85
  457.2 123.6 %fusion.9 = f32[128,4,2,4,256]{4,3,2,1,0:T(4,128)S(1)} fusion(s32[128]{0:T(128)S(1)} %add_add_fusion, s32[256,256]{1,0:T(8,128)S(1)} %iota_multiply_fusion, bf16[4,256,2,4,128]{1,0,3,2,4:T(4,128)(2,1)S(1)} %fusion.43), kind=kOutput, calls=%fused_computation.15 | convolution fusion | flops 671088640 | bytes 6554112 | tf_op jit(solution)/shard_map/cbr,erpsc->ebpsc/dot_general | solution.py:86
  584.4 124.8 %fusion.5 = f32[128,4,2,4,256]{4,3,2,1,0:T(4,128)S(1)} fusion(s32[128]{0:T(128)S(1)} %add_add_fusion, s32[256,256]{1,0:T(8,128)S(1)} %iota_multiply_fusion, bf16[4,256,2,4,128]{1,0,3,2,4:T(4,128)(2,1)S(1)} %fusion.42), kind=kOutput, calls=%fused_computation.13 | convolution fusion | flops 671088640 | bytes 6554112 | tf_op jit(solution)/shard_map/cbr,erpsc->ebpsc/dot_general | solution.py:86
  709.3 126.3 %add_reduce_fusion = bf16[128,4,4,256]{3,2,1,0:T(4,128)(2,1)S(1)} fusion(f32[128,4,2,4,256]{4,3,2,1,0:T(4,128)S(1)} %fusion.9, f32[128,4,2,4,256]{4,3,2,1,0:T(4,128)S(1)} %fusion.5, f32[128,4,2,4,256]{4,3,2,1,0:T(4,128)S(1)} %fusion.7, s32[128]{0:T(128)S(1)} %add_add_fusion, s32[256,256]{1,0:T(8,128)S(1)} %iota_multiply_fusion, ...), kind=kOutput, calls=%fused_computation.53 | convolution fusion | flops 676855808 | bytes 15991296 | tf_op jit(solution)/shard_map/cbr,erpsc->ebpsc/dot_general | solution.py:85
  837.4 29.0 %all_to_all.54 = bf16[1024,4,128]{2,1,0:T(4,128)(2,1)S(1)} all-to-all(bf16[1024,4,128]{2,1,0:T(4,128)(2,1)S(1)} %copy.123), channel_id=1, replica_groups=mesh['tm'=4,'feed'=8] {'feed'}, dimensions={0} | all-to-all | bytes 2097152 | tf_op jit(solution)/shard_map/all_to_all | solution.py:128
  870.6 50.7 %all-gather.2.cloned.1.call-done = bf16[128,16,1024]{2,0,1:T(8,128)(2,1)} async-done(((bf16[128,4,1024]{2,0,1:T(8,128)(2,1)}), bf16[128,16,1024]{2,0,1:T(8,128)(2,1)}) %all-gather.2.cloned.1.call-update) | async-done | bytes 4194320 | tf_op jit(solution)/shard_map/all_gather | solution.py:136
  927.0 56.3 %fusion.34 = f32[4,512,128]{2,1,0:T(8,128)S(1)} fusion(s32[1024,512]{0,1:T(8,128)S(1)} %copy.106, s32[4]{0:T(128)S(1)} %iota_add_fusion, bf16[128,4,1024]{2,1,0:T(4,128)(2,1)S(1)} %get-tuple-element.5), kind=kOutput, calls=%fused_computation.59 | convolution fusion | flops 568328192 | bytes 4194320 | tf_op jit(solution)/shard_map/vuw,uwt->vut/dot_general | solution.py:148
  983.3 56.3 %fusion.33 = f32[4,512,128]{2,1,0:T(8,128)S(1)} fusion(s32[1024,512]{0,1:T(8,128)S(1)} %copy.106, s32[4]{0:T(128)S(1)} %iota_add_fusion, bf16[128,4,1024]{2,1,0:T(4,128)(2,1)S(1)} %get-tuple-element.6), kind=kOutput, calls=%fused_computation.58 | convolution fusion | flops 568328192 | bytes 4194320 | tf_op jit(solution)/shard_map/vuw,uwt->vut/dot_general | solution.py:149
  1039.5 57.3 %fusion.51 = f32[128,1,4,512]{0,3,2,1:T(8,128)S(1)} fusion(f32[4,512,128]{2,1,0:T(8,128)S(1)} %fusion.34, s32[1024,512]{0,1:T(8,128)S(1)} %copy.106, s32[4]{0:T(128)S(1)} %iota_add_fusion, bf16[128,4,1024]{2,1,0:T(4,128)(2,1)S(1)} %get-tuple-element.6), kind=kOutput, calls=%fused_computation.77 | convolution fusion | flops 568590336 | bytes 5242896 | tf_op jit(solution)/shard_map/vuw,uwt->vut/dot_general | solution.py:148
  1096.8 32.6 %fusion.53 = f32[128,1,4,512]{0,3,2,1:T(8,128)S(1)} fusion(f32[4,512,128]{2,1,0:T(8,128)S(1)} %fusion.33, s32[1024,512]{0,1:T(8,128)S(1)} %copy.106, s32[4]{0:T(128)S(1)} %iota_add_fusion, bf16[128,4,1024]{2,1,0:T(4,128)(2,1)S(1)} %get-tuple-element.5), kind=kOutput, calls=%fused_computation.79 | convolution fusion | flops 568590336 | bytes 5242896 | tf_op jit(solution)/shard_map/vuw,uwt->vut/dot_general | solution.py:149
  1130.4 16.8 %all_to_all.55 = bf16[128,2,4,512]{0,2,1,3:T(4,128)(2,1)S(1)} all-to-all(bf16[128,2,4,512]{0,2,1,3:T(4,128)(2,1)S(1)} %copy.132), channel_id=1, replica_groups=mesh['tm'=4,'feed'=8] {'tm'}, dimensions={3} | all-to-all | bytes 2097152 | tf_op jit(solution)/shard_map/all_to_all | solution.py:153
  (50 shorter events, 69.8 us)
Async XLA Ops:
  19.6 2.0 copy-start
  24.9 72.5 %collective-permute-start = (bf16[256,3,2048]{2,0,1:T(8,128)(2,1)}, bf16[256,3,2048]{2,0,1:T(8,128)(2,1)}, u32[]{:S(2)}, u32[]{:S(2)}) collective-permute-start(bf16[256,3,2048]{2,0,1:T(8,128)(2,1)} %copy.109), channel_id=1, source_target_pairs={{0,8},{8,16},{16,24},{1,9},{9,17},{17,25},{2,10},{10,18},{18,26},{... | collective-permute-start | bytes 9437192 | tf_op jit(solution)/shard_map/ppermute | solution.py:22
  145.7 21.4 %copy-start.1 = (s32[2048]{0:T(1024)S(1)}, s32[2048]{0:T(1024)}, u32[]{:S(2)}) copy-start(s32[2048]{0:T(1024)} %param.6) | copy-start | bytes 24580
  145.7 22.2 %copy-start.3 = (s32[4]{0:T(128)S(1)}, s32[4]{0:T(128)}, u32[]{:S(2)}) copy-start(s32[4]{0:T(128)} %param.7) | copy-start | bytes 52
  145.7 22.2 %copy-start.2 = (s32[256]{0:T(256)S(1)}, s32[256]{0:T(256)}, u32[]{:S(2)}) copy-start(s32[256]{0:T(256)} %param.8) | copy-start | bytes 3076
  161.9 99.0 %all-to-all-start = ((bf16[256,4,2,1024]{0,2,1,3:T(2,128)(2,1)}), bf16[256,4,2,1024]{0,2,1,3:T(2,128)(2,1)}, u32[]{:S(2)}, u32[]{:S(2)}) async-start(bf16[256,4,2,1024]{0,2,1,3:T(2,128)(2,1)} %copy.112), calls=%async_computation | async-start | bytes 8388608 | tf_op jit(solution)/shard_map/all_to_all | solution.py:121
  166.7 754.6 %all-gather.2.cloned.1.call-start = ((), (), s32[]{:S(2)}) async-start(), calls=%async_computation.3 | async-start | bytes 5242880 | tf_op jit(solution)/shard_map/all_gather | solution.py:136
Sparse Core Ops, SparseCore 0:
  868.7 52.5 all-gather.1
where the time goes:
time: 1170 us; the launch traced here: 1160 us
  matrix products  746 us (64%)
  waiting for transfers between devices  174 us (15%)
  local copies, waits for them, and re-layouts  114 us (10%)
  other arithmetic  52.6 us (4%)
  blocking collectives  45.9 us (4%)
  between operations  14.1 us (1%)
    dot_general x2, matrix products, form_beams(): beam_real = north_mix(ns_real, east_real) - north_mix(ns_imag, east_imag)  263 us
    dot_general x2, matrix products, form_beams(): beam_imag = north_mix(ns_real, east_imag) + north_mix(ns_imag, east_real)  248 us
    all_to_all x1, waiting for transfers between devices, local(): lax.all_to_all(spectra, 'feed', split_axis=3, concat_axis=0, tiled=True)  92.8 us
    dot_general x1, matrix products, local(): shift_mixture(spec_imag, phase_imag)  57.3 us
    dot_general x1, matrix products, local(): shift_mixture(spec_real, phase_real) - shift_mixture(spec_imag, phase_imag)  56.3 us
    dot_general x1, matrix products, local(): shift_mixture(spec_imag, phase_real)  56.3 us
    all_gather x1, waiting for transfers between devices, local(): lax.all_gather(by_beam, 'tm', axis=1, tiled=True)  50.7 us
    another operation x2, other arithmetic  35.3 us
  transfers between devices with their start and end apart: 3, of which 3 were waited for; matrix products, arithmetic and copies ran while one was open for 3% of the time, Pallas kernels for 0%

commit v1 on v0

--- a/solution.py
+++ b/solution.py
@@ -3,7 +3,10 @@
 
 import jax
 import jax.numpy as jnp
+import numpy as np
 from jax import lax
+from jax.experimental import pallas as pl
+from jax.experimental.pallas import tpu as pltpu
 from jax.sharding import PartitionSpec as P
 
 NFFT = 2048
@@ -88,7 +91,7 @@
     return beam_power.reshape(-1, item_count, chan_count).astype(jnp.bfloat16)
 
 
-def local(voltages, feed_at_grid_slot, ew_grid, ns_grid, delays):
+def local_unaligned(voltages, feed_at_grid_slot, ew_grid, ns_grid, delays):
     feed_dev = voltages.shape[0]
     spec_dev = voltages.shape[1] // NFFT
     time_extent = lax.axis_size("tm")
@@ -154,7 +157,421 @@
     return jnp.einsum("brkd,rkt->dbt", combined, time_table, preferred_element_type=jnp.float32)
 
 
+MESH = pl.DeviceIdType.MESH
+
+
+def sincos(phases, modulus):
+    quarter = modulus // 4
+    quadrant = (phases + quarter // 2) >> (quarter.bit_length() - 1)
+    rest = (phases - quadrant * quarter).astype(jnp.float32) * (TWO_PI / modulus)
+    square = rest * rest
+    sine = rest * (
+        1.0 + square * (-1.0 / 6 + square * (1.0 / 120 + square * (-1.0 / 5040 + square / 362880)))
+    )
+    cosine = 1.0 + square * (
+        -0.5 + square * (1.0 / 24 + square * (-1.0 / 720 + square * (1.0 / 40320)))
+    )
+    swap = quadrant & 1 == 1
+    first = jnp.where(swap, sine, cosine)
+    second = jnp.where(swap, cosine, sine)
+    turned = quadrant & 3
+    return (
+        jnp.where((turned == 1) | (turned == 2), -first, first),
+        jnp.where(turned >= 2, -second, second),
+    )
+
+
+def window_constant(tap_count, series_length):
+    points = np.arange(tap_count * series_length, dtype=np.float64) + 0.5
+    offset = points / series_length - tap_count / 2.0
+    taper = 0.5 - 0.5 * np.cos(TWO_PI * points / (tap_count * series_length))
+    values = (np.sinc(offset) * taper).reshape(tap_count, series_length)
+    values = values / np.sqrt(np.sum(values * values, axis=0, keepdims=True))
+    return (values / 64.0).astype(np.float32)
+
+
+def dft_constant(series_length, columns, blocks):
+    product = np.outer(np.arange(columns), np.arange(series_length)) % series_length
+    angles = product * (TWO_PI / series_length)
+    factor = 1.0 / math.sqrt(series_length)
+    table = np.stack([np.cos(angles) * factor, -np.sin(angles) * factor])
+    table = table.reshape(2, blocks, columns // blocks, series_length).transpose(1, 0, 2, 3)
+    return table.reshape(blocks, -1, series_length).astype(jnp.bfloat16)
+
+
+def search_kernel(
+    volt, window, twiddle, placed, steer, rot, out,
+    raw, frames, hist, filtered, send, spec, placed_v, grid, east, rot_v, power, beams,
+    raw_s, placed_s, rot_s, hist_ss, hist_rs, spec_ss, spec_rs, beam_ss, beam_rs,
+):
+    spec_dev, feed_dev, length = frames.shape
+    feed_size = spec.shape[1]
+    chan_dev = spec.shape[2] // 2
+    tm_size = out.shape[0]
+    beam_dev, ns_beams = out.shape[3], power.shape[3]
+    pairs = power.shape[2]
+    ews = pairs // 2
+    tm = lax.axis_index("tm")
+    feed = lax.axis_index("feed")
+    after = lax.rem(tm + 1, tm_size)
+
+    def other_device(step):
+        other = lax.rem(tm * feed_size + feed + step, tm_size * feed_size)
+        return other // feed_size, lax.rem(other, feed_size)
+
+    barrier = pltpu.get_barrier_semaphore()
+
+    def greet(step, _):
+        pl.semaphore_signal(barrier, inc=1, device_id=other_device(step), device_id_type=MESH)
+        return 0
+
+    lax.fori_loop(1, tm_size * feed_size, greet, 0)
+
+    def raw_copy(s):
+        return pltpu.make_async_copy(
+            volt.at[:, pl.ds(s * length, length)], raw.at[s % 2], raw_s.at[s % 2]
+        )
+
+    placed_copy = pltpu.make_async_copy(placed, placed_v, placed_s)
+    rot_copy = pltpu.make_async_copy(rot, rot_v, rot_s)
+    raw_copy(spec_dev - 1).start()
+    raw_copy(spec_dev - 2).start()
+
+    step_rows = 16
+
+    def convert(s):
+        def body(i, _):
+            rows = pl.ds(pl.multiple_of(i * step_rows, step_rows), step_rows)
+            frames[s, rows, :] = raw[s % 2, rows, :].astype(jnp.float32).astype(jnp.bfloat16)
+            return 0
+
+        raw_copy(s).wait()
+        lax.fori_loop(0, feed_dev // step_rows, body, 0)
+        if s >= 2:
+            raw_copy(s - 2).start()
+
+    def history(i):
+        return pltpu.make_async_remote_copy(
+            src_ref=frames.at[spec_dev - TAPS + 1 + i],
+            dst_ref=hist.at[i],
+            send_sem=hist_ss.at[i],
+            recv_sem=hist_rs.at[i],
+            device_id=(after, feed),
+            device_id_type=MESH,
+        )
+
+    convert(spec_dev - 1)
+    pl.semaphore_wait(barrier, tm_size * feed_size - 1)
+    history(TAPS - 2).start()
+    for s in range(spec_dev - 2, -1, -1):
+        convert(s)
+        if s >= spec_dev - TAPS + 1:
+            history(s - (spec_dev - TAPS + 1)).start()
+    placed_copy.start()
+    rot_copy.start()
+
+    live = jnp.where(tm > 0, 1.0, 0.0).astype(jnp.float32)
+
+    def spec_copy(s, other, slot):
+        return pltpu.make_async_remote_copy(
+            src_ref=send.at[s, other],
+            dst_ref=spec.at[s, slot],
+            send_sem=spec_ss.at[s, other],
+            recv_sem=spec_rs.at[s, slot],
+            device_id=(tm, other),
+            device_id_type=MESH,
+        )
+
+    def channelize(s):
+        if s < TAPS - 1:
+            history(s).wait_recv()
+
+        def filter_rows(i, _):
+            rows = pl.ds(pl.multiple_of(i * step_rows, step_rows), step_rows)
+            total = None
+            for tap in range(TAPS):
+                at = s + tap - (TAPS - 1)
+                weights = window[tap : tap + 1, :]
+                if at < 0:
+                    term = hist[TAPS - 1 + at, rows, :].astype(jnp.float32) * (weights * live)
+                else:
+                    term = frames[at, rows, :].astype(jnp.float32) * weights
+                total = term if total is None else total + term
+            filtered[rows, :] = total.astype(jnp.bfloat16)
+            return 0
+
+        lax.fori_loop(0, feed_dev // step_rows, filter_rows, 0)
+
+        def transform(i, _):
+            other = lax.rem(feed + 1 + i, feed_size)
+            block = lax.dot_general(
+                twiddle[other],
+                filtered[...],
+                (((1,), (1,)), ((), ())),
+                preferred_element_type=jnp.float32,
+            ).astype(jnp.bfloat16)
+
+            @pl.when(other != feed)
+            def _():
+                send[s, other] = block
+                spec_copy(s, other, feed).start()
+
+            @pl.when(other == feed)
+            def _():
+                spec[s, other] = block
+
+            return 0
+
+        lax.fori_loop(0, feed_size, transform, 0)
+
+    def arrive(s):
+        def body(step, _):
+            other = lax.rem(feed + step, feed_size)
+            spec_copy(s, other, other).wait()
+            return 0
+
+        lax.fori_loop(1, feed_size, body, 0)
+
+    def place(s):
+        def body(m, _):
+            total = jnp.zeros(grid.shape[1:], jnp.float32)
+            for j in range(feed_size):
+                total += jnp.dot(
+                    spec[s, j],
+                    placed_v[m, j * feed_dev : (j + 1) * feed_dev, :],
+                    preferred_element_type=jnp.float32,
+                )
+            grid[m] = total
+            return 0
+
+        lax.fori_loop(0, grid.shape[0], body, 0)
+
+    def mix_east(at):
+        def body(i, _):
+            start = pl.multiple_of(i * 8, 8)
+            rows = pl.ds(start, 8)
+            rows_im = pl.ds(pl.multiple_of(chan_dev + start, 8), 8)
+            for pol in range(2):
+                re = [grid[2 * y + pol, rows, :] for y in range(4)]
+                im = [grid[2 * y + pol, rows_im, :] for y in range(4)]
+                for e in range(ews):
+                    sum_re = sum_im = None
+                    for y in range(4):
+                        w = e * 4 + y
+                        w_re = steer[rows, w : w + 1]
+                        w_im = steer[rows, 4 * ews + w : 4 * ews + w + 1]
+                        term_re = w_re * re[y] - w_im * im[y]
+                        term_im = w_re * im[y] + w_im * re[y]
+                        sum_re = term_re if sum_re is None else sum_re + term_re
+                        sum_im = term_im if sum_im is None else sum_im + term_im
+                    row = at * 2 * pairs + pol * ews + e
+                    east[rows, row, :] = sum_re
+                    east[rows, row + pairs, :] = sum_im
+            return 0
+
+        lax.fori_loop(0, chan_dev // 8, body, 0)
+
+    def mix_north(count):
+        def body(c, _):
+            coarse_re, coarse_im, fine_re, fine_im = (rot_v[k, c] for k in range(4))
+            parts_re, parts_im = [], []
+            for r in range(coarse_re.shape[0]):
+                a_re, a_im = coarse_re[r : r + 1, :], coarse_im[r : r + 1, :]
+                parts_re.append((a_re * fine_re - a_im * fine_im).astype(jnp.bfloat16))
+                parts_im.append((a_re * fine_im + a_im * fine_re).astype(jnp.bfloat16))
+            side = east[c, : count * 2 * pairs, :].astype(jnp.bfloat16)
+            by_re = jnp.dot(
+                side, jnp.concatenate(parts_re, axis=0), preferred_element_type=jnp.float32
+            )
+            by_im = jnp.dot(
+                side, jnp.concatenate(parts_im, axis=0), preferred_element_type=jnp.float32
+            )
+            for k in range(count):
+                lo, mid, hi = 2 * k * pairs, (2 * k + 1) * pairs, (2 * k + 2) * pairs
+                beam_re = by_re[lo:mid] - by_im[mid:hi]
+                beam_im = by_re[mid:hi] + by_im[lo:mid]
+                power[k, c] = beam_re * beam_re + beam_im * beam_im
+            return 0
+
+        lax.fori_loop(0, chan_dev, body, 0)
+
+    def transpose_power(s, k):
+        width = beam_dev * tm_size
+        for e in range(ews):
+            total = power[k, :, e, :] + power[k, :, ews + e, :]
+            turned = total.T.astype(jnp.bfloat16)
+            for part in range(ns_beams // beam_dev):
+                first = e * ns_beams + part * beam_dev
+                block = turned[part * beam_dev : (part + 1) * beam_dev]
+                beams[first % width // beam_dev, first // width, s] = block
+
+    def beam_copy(first, last, group, peer, slot):
+        return pltpu.make_async_remote_copy(
+            src_ref=beams.at[peer[0], peer[1], pl.ds(first, last - first)],
+            dst_ref=out.at[slot[0], slot[1], pl.ds(first, last - first)],
+            send_sem=beam_ss.at[group, peer[0], peer[1]],
+            recv_sem=beam_rs.at[group, slot[0], slot[1]],
+            device_id=peer,
+            device_id_type=MESH,
+        )
+
+    groups = [(spec_dev - 1, 1), (0, 0)] if spec_dev > 1 else [(0, 0)]
+
+    def form(group):
+        high, low = groups[group]
+        for k, s in enumerate(range(low, high + 1)):
+            place(s)
+            mix_east(k)
+        mix_north(high + 1 - low)
+        for k, s in enumerate(range(low, high + 1)):
+            transpose_power(s, k)
+
+        def go(step, _):
+            beam_copy(low, high + 1, group, other_device(step), (tm, feed)).start()
+            return 0
+
+        lax.fori_loop(1, tm_size * feed_size, go, 0)
+        out[tm, feed, low : high + 1] = beams[tm, feed, low : high + 1]
+
+    for s in range(spec_dev - 1, -1, -1):
+        channelize(s)
+    placed_copy.wait()
+    rot_copy.wait()
+    for group, (high, low) in enumerate(groups):
+        for s in range(high, low - 1, -1):
+            arrive(s)
+        form(group)
+    for group, (high, low) in enumerate(groups):
+        def finish(step, _):
+            peer = other_device(step)
+            beam_copy(low, high + 1, group, peer, peer).wait()
+            return 0
+
+        lax.fori_loop(1, tm_size * feed_size, finish, 0)
+    for i in range(TAPS - 1):
+        history(i).wait_send()
+
+
+def search(voltages, placed, steer, rot, tm_size, feed_size, beam_dev):
+    feed_dev = voltages.shape[0]
+    spec_dev = voltages.shape[1] // NFFT
+    chan_dev = CHANS // feed_size
+    ns_beams = rot.shape[3]
+    pairs = 2 * steer.shape[1] // 8
+    window = jnp.asarray(window_constant(TAPS, NFFT))
+    twiddle = jnp.asarray(dft_constant(NFFT, CHANS, feed_size))
+    blocks = (spec_dev, feed_size, 2 * chan_dev, feed_dev)
+    batch = max(spec_dev - 1, 1)
+    vmem = pl.BlockSpec(memory_space=pltpu.VMEM)
+    hbm = pl.BlockSpec(memory_space=pl.ANY)
+    dma = pltpu.SemaphoreType.DMA
+    sent = (tm_size, feed_size, spec_dev, beam_dev, chan_dev)
+    return pl.pallas_call(
+        search_kernel,
+        out_shape=jax.ShapeDtypeStruct(sent, jnp.bfloat16),
+        in_specs=[hbm, vmem, vmem, hbm, vmem, hbm],
+        out_specs=vmem,
+        scratch_shapes=[
+            pltpu.VMEM((2, feed_dev, NFFT), jnp.int32),
+            pltpu.VMEM((spec_dev, feed_dev, NFFT), jnp.bfloat16),
+            pltpu.VMEM((TAPS - 1, feed_dev, NFFT), jnp.bfloat16),
+            pltpu.VMEM((feed_dev, NFFT), jnp.bfloat16),
+            pltpu.VMEM(blocks, jnp.bfloat16),
+            pltpu.VMEM(blocks, jnp.bfloat16),
+            pltpu.VMEM(placed.shape, jnp.bfloat16),
+            pltpu.VMEM((placed.shape[0], 2 * chan_dev, placed.shape[2]), jnp.float32),
+            pltpu.VMEM((chan_dev, batch * 2 * pairs, ROWS), jnp.float32),
+            pltpu.VMEM(rot.shape, jnp.float32),
+            pltpu.VMEM((batch, chan_dev, pairs, ns_beams), jnp.float32),
+            pltpu.VMEM(sent, jnp.bfloat16),
+            dma((2,)),
+            dma(()),
+            dma(()),
+            dma((TAPS - 1,)),
+            dma((TAPS - 1,)),
+            dma((spec_dev, feed_size)),
+            dma((spec_dev, feed_size)),
+            dma((2, tm_size, feed_size)),
+            dma((2, tm_size, feed_size)),
+        ],
+        compiler_params=pltpu.CompilerParams(
+            collective_id=0, has_side_effects=True, vmem_limit_bytes=60 * 1024 * 1024
+        ),
+        name="search",
+    )(voltages, window, twiddle, placed, steer, rot)
+
+
+def ns_rotations(ns_grid, chan_ids, stride):
+    coarse = jnp.arange(ROWS // stride, dtype=jnp.int32) * stride
+    fine = jnp.arange(stride, dtype=jnp.int32)
+    step = (ns_grid[None, :] * chan_ids[:, None]) & (phase_modulus - 1)
+    tables = []
+    for rows in (coarse, fine):
+        phases = (rows[None, :, None] * step[:, None, :]) & (phase_modulus - 1)
+        tables.append(sincos(phases, phase_modulus))
+    return tables
+
+
+def local(voltages, feed_at_grid_slot, ew_grid, ns_grid, delays):
+    spec_dev = voltages.shape[1] // NFFT
+    tm_size = lax.axis_size("tm")
+    feed_size = lax.axis_size("feed")
+    spec_total = spec_dev * tm_size
+    chan_dev = CHANS // feed_size
+    feeds = feed_at_grid_slot.shape[0]
+
+    slots = feed_at_grid_slot.reshape(ROWS, 8).T
+    placed = jnp.arange(feeds, dtype=jnp.int32)[None, :, None] == slots[:, None, :]
+    placed = placed.astype(jnp.bfloat16)
+
+    chan_ids = lax.axis_index("feed") * chan_dev + jnp.arange(chan_dev, dtype=jnp.int32) + CHANS
+    phases = (
+        jnp.arange(4, dtype=jnp.int32)[None, None, :]
+        * ew_grid[None, :, None]
+        * chan_ids[:, None, None]
+    ) & (phase_modulus - 1)
+    ew = [part.reshape(chan_dev, -1) * 0.5 for part in sincos(phases, phase_modulus)]
+    steer = jnp.concatenate(ew, axis=1).astype(jnp.bfloat16).astype(jnp.float32)
+
+    coarse, fine = ns_rotations(ns_grid, chan_ids, 16)
+    factor = 1.0 / math.sqrt(ROWS)
+    rot = jnp.stack([coarse[0] * factor, coarse[1] * factor, fine[0], fine[1]])
+
+    beam_dev = ew_grid.shape[0] * ns_grid.shape[0] // (tm_size * feed_size)
+    blocks = search(voltages, placed, steer, rot, tm_size, feed_size, beam_dev)
+    by_beam = blocks.transpose(0, 2, 3, 1, 4).reshape(spec_total, beam_dev, CHANS)
+
+    half = spec_total // 2
+    factor = 1.0 / math.sqrt(spec_total)
+    freq_ids = np.arange(1, half + 1)
+    turn = np.outer(freq_ids, np.arange(spec_total)) % spec_total * (TWO_PI / spec_total)
+    table = np.stack([np.cos(turn), -np.sin(turn)]) * factor
+    time_table = jnp.asarray(table.astype(jnp.bfloat16))
+    spectrum = jnp.einsum("rkt,tbc->krbc", time_table, by_beam, preferred_element_type=jnp.float32)
+    spectrum = spectrum.astype(jnp.bfloat16).reshape(half, 2 * beam_dev, CHANS)
+    base_re, base_im = sincos(delays & (spec_total - 1), spec_total)
+    powers_re, powers_im = [base_re], [base_im]
+    for _ in range(1, half):
+        re, im = powers_re[-1], powers_im[-1]
+        powers_re.append(re * base_re - im * base_im)
+        powers_im.append(re * base_im + im * base_re)
+    phase = jnp.stack([jnp.stack(powers_re), jnp.stack(powers_im)], axis=2).astype(jnp.bfloat16)
+    phase = phase.reshape(half, CHANS, -1)
+    moved = jnp.einsum("kmc,kcd->kmd", spectrum, phase, preferred_element_type=jnp.float32)
+    moved = moved.reshape(half, 2, beam_dev, 2, -1)
+    moved_real = moved[:, 0, :, 0] - moved[:, 1, :, 1]
+    moved_imag = moved[:, 0, :, 1] + moved[:, 1, :, 0]
+    folded = jnp.stack([moved_real, moved_imag]) * (1.0 / math.sqrt(CHANS))
+    folded = folded.astype(jnp.bfloat16)
+    combined = lax.all_to_all(folded, "tm", split_axis=3, concat_axis=2, tiled=True)
+    weight = np.where(2 * freq_ids == spec_total, 1.0, 2.0)[None, :, None]
+    back = jnp.asarray((table.astype(jnp.bfloat16).astype(np.float64) * weight).astype(jnp.bfloat16))
+    return jnp.einsum("rkbd,rkt->dbt", combined, back, preferred_element_type=jnp.float32)
+
+
 def solution(mesh):
     in_specs = (P("feed", "tm"), P(), P(), P(), P())
     out_specs = P("tm", "feed", None)
-    return jax.shard_map(local, mesh=mesh, in_specs=in_specs, out_specs=out_specs, check_vma=False)
+    aligned = CHANS // mesh.shape["feed"] % 128 == 0
+    body = local if aligned else local_unaligned
+    return jax.shard_map(body, mesh=mesh, in_specs=in_specs, out_specs=out_specs, check_vma=False)

time: 1170 us -> 297 us (0.25)
  matrix products: 746 us -> 3.77 us
  Pallas kernels: 0 us -> 176 us
  waiting for transfers between devices: 174 us -> 0 us
  local copies, waits for them, and re-layouts: 114 us -> 25.1 us
  blocking collectives: 45.9 us -> 11.8 us
  other arithmetic: 52.6 us -> 76.3 us
  between operations: 14.1 us -> 0.53 us
    dot_general x15 -> x3, matrix products: 746 us -> 3.77 us  [the longest x1 3.02 us: local(): jnp.einsum('kmc,kcd->kmd', spectrum, phase, preferred_element_type=jnp.fl...]
    pallas_call x0 -> x1, Pallas kernels: none -> 176 us  [search(): pl.pallas_call(search_kernel, out_shape=jax.ShapeDtypeStruct(sent, jnp.bf...]
    all_to_all x1 -> x0, waiting for transfers between devices: 92.8 us -> none  [local(): lax.all_to_all(spectra, 'feed', split_axis=3, concat_axis=0, tiled=True)]
    all_gather x1 -> x0, waiting for transfers between devices: 50.7 us -> none  [local(): lax.all_gather(by_beam, 'tm', axis=1, tiled=True)]
    unnamed x0 -> x13, other arithmetic: none -> 48.3 us
    ppermute x1 -> x0, waiting for transfers between devices: 30 us -> none  [from_behind(): return lax.ppermute(block, axis, route)]
    all_to_all x1 -> x0, blocking collectives: 29 us -> none  [local(): lax.all_to_all(intensity, 'feed', split_axis=0, concat_axis=2, tiled=True)]
    gather x2 -> x0, local copies, waits for them, and re-layouts: 27.7 us -> none  [form_beams(): jnp.take(block_in, feed_at_grid_slot, axis=0)]
  transfers between devices with their start and end apart: 3 -> 0, of which waited for: 3 -> 0; matrix products, arithmetic and copies ran while one was open for 3% -> 0% of each run, Pallas kernels for 0% -> 0%
where the time goes in v1:
time: 297 us; the launch traced here: 294 us
  Pallas kernels  176 us (59%)
  other arithmetic  76.3 us (26%)
  local copies, waits for them, and re-layouts  25.1 us (8%)
  blocking collectives  11.8 us (4%)
  matrix products  3.77 us (1%)
    pallas_call x1, Pallas kernels, search(): pl.pallas_call(search_kernel, out_shape=jax.ShapeDtypeStruct(sent, jnp.bf...  176 us
    unnamed x13, other arithmetic  48.3 us
    all_to_all x1, blocking collectives, local(): lax.all_to_all(folded, 'tm', split_axis=3, concat_axis=2, tiled=True)  11.8 us
    convert_element_type x1, other arithmetic, local(): placed = placed.astype(jnp.bfloat16)  6.21 us

profile of v1, /device:TPU:0, one launch (start us, length us, event | category | flops | bytes accessed | tf_op | source)
XLA Modules:
  0.0 293.7 jit_solution(5981054200184621590)
XLA Ops:
  3.4 6.2 %fusion.placed = bf16[8,2048,256]{2,1,0:T(8,128)(2,1)} fusion(s32[8,256]{1,0:T(8,128)S(1)} %copy.62), kind=kLoop, calls=%fused_computation.2 | loop fusion | flops 8388608 | bytes 8396800 | tf_op jit(solution)/shard_map/convert_element_type | solution.py:525
  9.6 5.6 %fusion.1 = (f32[1,128,16,256]{3,2,1,0:T(8,128)S(1)}, f32[1,128,16,256]{3,2,1,0:T(8,128)S(1)}, f32[1,128,16,256]{3,2,1,0:T(8,128)S(1)}, f32[1,128,16,256]{3,2,1,0:T(8,128)S(1)}) fusion(s32[128,256]{1,0:T(8,128)S(1)} %multiply_and_fusion.2, s32[16]{0:T(128)S(1)} %iota_multiply_fusion), kind=kLoop, calls=%fused_computation.13 | loop fusion | flops 41943040 | bytes 8519744 | tf_op jit(solution)/shard_map/mul | solution.py:538
  15.2 3.7 %pad_maximum_fusion.rot = f32[4,128,16,256]{3,2,1,0:T(8,128)} fusion(f32[1,128,16,256]{3,2,1,0:T(8,128)S(1)} %get-tuple-element.16, f32[1,128,16,256]{3,2,1,0:T(8,128)S(1)} %get-tuple-element.15, f32[1,128,16,256]{3,2,1,0:T(8,128)S(1)} %get-tuple-element.14, f32[1,128,16,256]{3,2,1,0:T(8,128)S(1)} %get-tuple-element.13), kind=kLoop, calls=%fused_computation.3 | loop fusion | flops 6291456 | bytes 16777216 | tf_op jit(solution)/shard_map/stack | solution.py:538
  18.9 176.3 %search.1 = bf16[4,8,4,32,128]{4,3,2,1,0:T(8,128)(2,1)} custom-call(s32[256,8192]{1,0:T(8,128)} %volt.1, f32[4,2048]{1,0:T(4,128)} %constant.58.clone.window, bf16[8,256,2048]{2,1,0:T(8,128)(2,1)} %constant.59.clone.twiddle, bf16[8,2048,256]{2,1,0:T(8,128)(2,1)} %fusion.placed, f32[128,32]{1,0:T(8,128)} %copy.63.steer, f32[4,128,16,256]{3,2,1,0:T(8,128)} %pad_maximum_fusion.rot), custom_call_target="tpu_custom_call" | custom-call | tf_op jit(solution)/shard_map/search/pallas_call | solution.py:469
  199.5 2.3 bitcast_dynamic-update-slice_fusion.8
  201.8 2.8 fusion.43
  204.7 3.2 %fusion.31 = bf16[8,1024,512]{2,1,0:T(8,128)(2,1)S(1)} fusion(bf16[8,1024,512]{2,1,0:T(8,128)(2,1)S(1)} %fusion.43, s32[1024,512]{1,0:T(8,128)S(1)} %copy-done), kind=kLoop, calls=%fused_computation.79 | loop fusion | flops 24641536 | bytes 3145728
  207.9 3.6 %bitcast_dynamic-update-slice_fusion.7 = bf16[8,1024,512]{2,1,0:T(8,128)(2,1)S(1)} fusion(bf16[8,1024,512]{2,1,0:T(8,128)(2,1)S(1)} %fusion.31, s32[1024,512]{1,0:T(8,128)S(1)} %copy-done), kind=kLoop, calls=%fused_computation.101 | loop fusion | flops 27787264 | bytes 3145728
  211.4 4.0 %bitcast_dynamic-update-slice_fusion.6 = bf16[8,1024,512]{2,1,0:T(8,128)(2,1)S(1)} fusion(bf16[8,1024,512]{2,1,0:T(8,128)(2,1)S(1)} %bitcast_dynamic-update-slice_fusion.7, s32[1024,512]{1,0:T(8,128)S(1)} %copy-done), kind=kLoop, calls=%fused_computation.100 | loop fusion | flops 30932992 | bytes 3145728
  215.4 5.2 %fusion.39 = bf16[8,1024,512]{2,1,0:T(8,128)(2,1)S(1)} fusion(bf16[8,1024,512]{2,1,0:T(8,128)(2,1)S(1)} %bitcast_dynamic-update-slice_fusion.6, s32[1024,512]{1,0:T(8,128)S(1)} %copy-done), kind=kLoop, calls=%fused_computation.87 | loop fusion | flops 34078720 | bytes 3145728
  220.6 5.1 %fusion.41 = (bf16[8,1024,512]{2,1,0:T(8,128)(2,1)S(1)}, bf16[8,1024,512]{2,1,0:T(8,128)(2,1)S(1)}) fusion(bf16[8,1024,512]{2,1,0:T(8,128)(2,1)S(1)} %fusion.39, s32[1024,512]{1,0:T(8,128)S(1)} %copy-done), kind=kLoop, calls=%fused_computation.89 | loop fusion | flops 37748736 | bytes 4194304
  225.7 5.8 %bitcast_dynamic-update-slice_fusion.5 = (bf16[8,1024,512]{2,1,0:T(8,128)(2,1)S(1)}, bf16[8,1024,512]{2,1,0:T(8,128)(2,1)S(1)}) fusion(bf16[8,1024,512]{2,1,0:T(8,128)(2,1)S(1)} %get-tuple-element.11, s32[1024,512]{1,0:T(8,128)S(1)} %copy-done, bf16[8,1024,512]{2,1,0:T(8,128)(2,1)S(1)} %get-tuple-element.12), kind=kLoop, calls=%fused_computation.99 | loop fusion | flops 40894464 | bytes 4194304 | tf_op jit(solution)/shard_map/stack | solution.py:558
  231.5 3.2 %fusion.35 = bf16[8,1024,512]{2,1,0:T(8,128)(2,1)S(1)} fusion(bf16[8,1024,512]{2,1,0:T(8,128)(2,1)S(1)} %get-tuple-element.10, s32[1024,512]{1,0:T(8,128)S(1)} %copy-done), kind=kLoop, calls=%fused_computation.83 | loop fusion | flops 24641536 | bytes 3145728
  234.6 3.6 %bitcast_dynamic-update-slice_fusion.3 = bf16[8,1024,512]{2,1,0:T(8,128)(2,1)S(1)} fusion(bf16[8,1024,512]{2,1,0:T(8,128)(2,1)S(1)} %fusion.35, s32[1024,512]{1,0:T(8,128)S(1)} %copy-done), kind=kLoop, calls=%fused_computation.97 | loop fusion | flops 27787264 | bytes 3145728
  238.2 4.0 %bitcast_dynamic-update-slice_fusion.2 = bf16[8,1024,512]{2,1,0:T(8,128)(2,1)S(1)} fusion(bf16[8,1024,512]{2,1,0:T(8,128)(2,1)S(1)} %bitcast_dynamic-update-slice_fusion.3, s32[1024,512]{1,0:T(8,128)S(1)} %copy-done), kind=kLoop, calls=%fused_computation.96 | loop fusion | flops 30932992 | bytes 3145728
  242.2 4.8 %bitcast_dynamic-update-slice_fusion.1 = bf16[8,1024,512]{2,1,0:T(8,128)(2,1)S(1)} fusion(bf16[8,1024,512]{2,1,0:T(8,128)(2,1)S(1)} %bitcast_dynamic-update-slice_fusion.2, s32[1024,512]{1,0:T(8,128)S(1)} %copy-done), kind=kLoop, calls=%fused_computation.95 | loop fusion | flops 34078720 | bytes 3145728
  247.0 5.1 %fusion.37 = bf16[8,1024,512]{2,1,0:T(8,128)(2,1)S(1)} fusion(bf16[8,1024,512]{2,1,0:T(8,128)(2,1)S(1)} %bitcast_dynamic-update-slice_fusion.1, s32[1024,512]{1,0:T(8,128)S(1)} %copy-done), kind=kLoop, calls=%fused_computation.85 | loop fusion | flops 37224448 | bytes 3145728
  252.1 5.5 %bitcast_dynamic-update-slice_fusion = bf16[8,1024,512]{2,1,0:T(8,128)(2,1)S(1)} fusion(bf16[8,1024,512]{2,1,0:T(8,128)(2,1)S(1)} %fusion.37, s32[1024,512]{1,0:T(8,128)S(1)} %copy-done), kind=kLoop, calls=%fused_computation.94 | loop fusion | flops 40370176 | bytes 3145728 | tf_op jit(solution)/shard_map/stack | solution.py:558
  259.2 2.3 copy.83
  261.5 3.0 %fusion.60 = f32[8,64,1024]{2,1,0:T(8,128)S(1)} fusion(bf16[8,64,1024]{2,1,0:T(8,128)(2,1)S(1)} %bitcast.92, bf16[8,1024,1024]{2,1,0:T(8,128)(2,1)S(1)} %bitcast.87), kind=kOutput, calls=%fused_computation.134 | convolution fusion | flops 1073741824 | bytes 19922944 | tf_op jit(solution)/shard_map/kmc,kcd->kmd/dot_general | solution.py:560
  264.6 2.8 reshape.363
  267.4 4.5 %fusion.59 = (f32[8,1,32,1,512]{4,3,2,1,0:T(1,128)S(1)}, f32[8,1,32,1,512]{4,3,2,1,0:T(1,128)S(1)}, f32[8,1,32,1,512]{4,3,2,1,0:T(1,128)S(1)}, f32[8,1,32,1,512]{4,3,2,1,0:T(1,128)S(1)}) fusion(f32[8,2,32,2,512]{4,3,2,1,0:T(2,128)} %reshape.363), kind=kLoop, calls=%fused_computation.133 | loop fusion | bytes 4194304 | tf_op jit(solution)/shard_map/slice | solution.py:562
  274.3 2.4 reshape.370
  276.7 11.8 %all_to_all.18 = bf16[4,2,32768]{2,1,0:T(2,128)(2,1)S(1)} all-to-all(bf16[4,2,32768]{2,1,0:T(2,128)(2,1)S(1)} %reshape.370), channel_id=1, replica_groups=mesh['tm'=4,'feed'=8] {'tm'}, dimensions={0} | all-to-all | bytes 1048576 | tf_op jit(solution)/shard_map/all_to_all | solution.py:566
  (31 shorter events, 16.6 us)
Async XLA Ops:
  195.2 2.7 copy-start.2
  197.9 1.6 copy-start
  288.5 3.1 %copy-start.1 = (bf16[2,8,16,1]{2,1,0,3:T(8,128)(2,1)S(1)}, bf16[2,8,16,1]{2,1,0,3:T(8,128)(2,1)}, u32[]{:S(2)}) copy-start(bf16[2,8,16,1]{2,1,0,3:T(8,128)(2,1)} %constant.10) | copy-start | bytes 1540

commit v2 on v1

--- a/solution.py
+++ b/solution.py
@@ -200,9 +200,9 @@
 
 
 def search_kernel(
-    volt, window, twiddle, placed, steer, rot, out,
-    raw, frames, hist, filtered, send, spec, placed_v, grid, east, rot_v, power, beams,
-    raw_s, placed_s, rot_s, hist_ss, hist_rs, spec_ss, spec_rs, beam_ss, beam_rs,
+    volt, window, twiddle_hbm, slots, ew_row, ns_row, out,
+    raw, frames, hist, filtered, send, spec, twiddle, placed_v, grid, east, steer, rot_v, power,
+    beams, raw_s, twiddle_s, hist_ss, hist_rs, spec_ss, spec_rs, beam_ss, beam_rs,
 ):
     spec_dev, feed_dev, length = frames.shape
     feed_size = spec.shape[1]
@@ -232,10 +232,10 @@
             volt.at[:, pl.ds(s * length, length)], raw.at[s % 2], raw_s.at[s % 2]
         )
 
-    placed_copy = pltpu.make_async_copy(placed, placed_v, placed_s)
-    rot_copy = pltpu.make_async_copy(rot, rot_v, rot_s)
+    twiddle_copy = pltpu.make_async_copy(twiddle_hbm, twiddle, twiddle_s)
     raw_copy(spec_dev - 1).start()
     raw_copy(spec_dev - 2).start()
+    twiddle_copy.start()
 
     step_rows = 16
 
@@ -267,8 +267,7 @@
         convert(s)
         if s >= spec_dev - TAPS + 1:
             history(s - (spec_dev - TAPS + 1)).start()
-    placed_copy.start()
-    rot_copy.start()
+    twiddle_copy.wait()
 
     live = jnp.where(tm > 0, 1.0, 0.0).astype(jnp.float32)
 
@@ -323,6 +322,39 @@
             return 0
 
         lax.fori_loop(0, feed_size, transform, 0)
+
+    def make_tables():
+        def one_hot(i, _):
+            rows = pl.ds(pl.multiple_of(i * step_rows, step_rows), step_rows)
+            shape = (step_rows, placed_v.shape[2])
+            feeds = lax.broadcasted_iota(jnp.int32, shape, 0) + i * step_rows
+            for m in range(placed_v.shape[0]):
+                hit = feeds == slots[m : m + 1, :]
+                placed_v[m, rows, :] = jnp.where(hit, 1.0, 0.0).astype(jnp.bfloat16)
+            return 0
+
+        lax.fori_loop(0, placed_v.shape[1] // step_rows, one_hot, 0)
+        first = feed * chan_dev + CHANS
+        chans = lax.broadcasted_iota(jnp.int32, (chan_dev, 4 * ews), 0) + first
+        turns = sincos((ew_row[...] * chans) & (phase_modulus - 1), phase_modulus)
+        for part, value in enumerate(turns):
+            value = (value * 0.5).astype(jnp.bfloat16).astype(jnp.float32)
+            steer[:, part * 4 * ews : (part + 1) * 4 * ews] = value
+        fine_rows = rot_v.shape[2]
+        row_ids = lax.broadcasted_iota(jnp.int32, (fine_rows, ns_beams), 0)
+        factor = 1.0 / math.sqrt(ROWS)
+
+        def rotations(c, _):
+            phases = row_ids * ((ns_row[...] * (first + c)) & (phase_modulus - 1))
+            fine = sincos(phases & (phase_modulus - 1), phase_modulus)
+            coarse = sincos((phases * fine_rows) & (phase_modulus - 1), phase_modulus)
+            rot_v[0, c] = coarse[0] * factor
+            rot_v[1, c] = coarse[1] * factor
+            rot_v[2, c] = fine[0]
+            rot_v[3, c] = fine[1]
+            return 0
+
+        lax.fori_loop(0, chan_dev, rotations, 0)
 
     def arrive(s):
         def body(step, _):
@@ -372,7 +404,7 @@
         lax.fori_loop(0, chan_dev // 8, body, 0)
 
     def mix_north(count):
-        def body(c, _):
+        def channel(c):
             coarse_re, coarse_im, fine_re, fine_im = (rot_v[k, c] for k in range(4))
             parts_re, parts_im = [], []
             for r in range(coarse_re.shape[0]):
@@ -391,9 +423,13 @@
                 beam_re = by_re[lo:mid] - by_im[mid:hi]
                 beam_im = by_re[mid:hi] + by_im[lo:mid]
                 power[k, c] = beam_re * beam_re + beam_im * beam_im
-            return 0
-
-        lax.fori_loop(0, chan_dev, body, 0)
+
+        def body(i, _):
+            for c in range(4):
+                channel(i * 4 + c)
+            return 0
+
+        lax.fori_loop(0, chan_dev // 4, body, 0)
 
     def transpose_power(s, k):
         width = beam_dev * tm_size
@@ -415,13 +451,12 @@
             device_id_type=MESH,
         )
 
-    groups = [(spec_dev - 1, 1), (0, 0)] if spec_dev > 1 else [(0, 0)]
+    groups = [(s, s) for s in range(min(spec_dev, 2) - 1, -1, -1)]
+    if spec_dev > 2:
+        groups = [(spec_dev - 1, 2)] + groups
 
     def form(group):
         high, low = groups[group]
-        for k, s in enumerate(range(low, high + 1)):
-            place(s)
-            mix_east(k)
         mix_north(high + 1 - low)
         for k, s in enumerate(range(low, high + 1)):
             transpose_power(s, k)
@@ -433,14 +468,21 @@
         lax.fori_loop(1, tm_size * feed_size, go, 0)
         out[tm, feed, low : high + 1] = beams[tm, feed, low : high + 1]
 
-    for s in range(spec_dev - 1, -1, -1):
+    def beamform(s):
+        for group, (high, low) in enumerate(groups):
+            if low <= s <= high:
+                arrive(s)
+                place(s)
+                mix_east(s - low)
+                if s == low:
+                    form(group)
+
+    channelize(spec_dev - 1)
+    make_tables()
+    for s in range(spec_dev - 2, -1, -1):
         channelize(s)
-    placed_copy.wait()
-    rot_copy.wait()
-    for group, (high, low) in enumerate(groups):
-        for s in range(high, low - 1, -1):
-            arrive(s)
-        form(group)
+        beamform(s + 1)
+    beamform(0)
     for group, (high, low) in enumerate(groups):
         def finish(step, _):
             peer = other_device(step)
@@ -452,16 +494,17 @@
         history(i).wait_send()
 
 
-def search(voltages, placed, steer, rot, tm_size, feed_size, beam_dev):
+def search(voltages, slots, ew_row, ns_row, tm_size, feed_size, beam_dev):
     feed_dev = voltages.shape[0]
     spec_dev = voltages.shape[1] // NFFT
     chan_dev = CHANS // feed_size
-    ns_beams = rot.shape[3]
-    pairs = 2 * steer.shape[1] // 8
+    ns_beams = ns_row.shape[1]
+    pairs = 2 * ew_row.shape[1] // 4
+    fine_rows = math.isqrt(ROWS)
     window = jnp.asarray(window_constant(TAPS, NFFT))
     twiddle = jnp.asarray(dft_constant(NFFT, CHANS, feed_size))
     blocks = (spec_dev, feed_size, 2 * chan_dev, feed_dev)
-    batch = max(spec_dev - 1, 1)
+    batch = max(spec_dev - 2, 1)
     vmem = pl.BlockSpec(memory_space=pltpu.VMEM)
     hbm = pl.BlockSpec(memory_space=pl.ANY)
     dma = pltpu.SemaphoreType.DMA
@@ -469,7 +512,7 @@
     return pl.pallas_call(
         search_kernel,
         out_shape=jax.ShapeDtypeStruct(sent, jnp.bfloat16),
-        in_specs=[hbm, vmem, vmem, hbm, vmem, hbm],
+        in_specs=[hbm, vmem, hbm, vmem, vmem, vmem],
         out_specs=vmem,
         scratch_shapes=[
             pltpu.VMEM((2, feed_dev, NFFT), jnp.int32),
@@ -478,95 +521,182 @@
             pltpu.VMEM((feed_dev, NFFT), jnp.bfloat16),
             pltpu.VMEM(blocks, jnp.bfloat16),
             pltpu.VMEM(blocks, jnp.bfloat16),
-            pltpu.VMEM(placed.shape, jnp.bfloat16),
-            pltpu.VMEM((placed.shape[0], 2 * chan_dev, placed.shape[2]), jnp.float32),
+            pltpu.VMEM(twiddle.shape, jnp.bfloat16),
+            pltpu.VMEM((slots.shape[0], slots.size, ROWS), jnp.bfloat16),
+            pltpu.VMEM((slots.shape[0], 2 * chan_dev, ROWS), jnp.float32),
             pltpu.VMEM((chan_dev, batch * 2 * pairs, ROWS), jnp.float32),
-            pltpu.VMEM(rot.shape, jnp.float32),
+            pltpu.VMEM((chan_dev, 2 * ew_row.shape[1]), jnp.float32),
+            pltpu.VMEM((4, chan_dev, fine_rows, ns_beams), jnp.float32),
             pltpu.VMEM((batch, chan_dev, pairs, ns_beams), jnp.float32),
             pltpu.VMEM(sent, jnp.bfloat16),
             dma((2,)),
-            dma(()),
             dma(()),
             dma((TAPS - 1,)),
             dma((TAPS - 1,)),
             dma((spec_dev, feed_size)),
             dma((spec_dev, feed_size)),
-            dma((2, tm_size, feed_size)),
-            dma((2, tm_size, feed_size)),
+            dma((3, tm_size, feed_size)),
+            dma((3, tm_size, feed_size)),
         ],
         compiler_params=pltpu.CompilerParams(
             collective_id=0, has_side_effects=True, vmem_limit_bytes=60 * 1024 * 1024
         ),
         name="search",
-    )(voltages, window, twiddle, placed, steer, rot)
-
-
-def ns_rotations(ns_grid, chan_ids, stride):
-    coarse = jnp.arange(ROWS // stride, dtype=jnp.int32) * stride
-    fine = jnp.arange(stride, dtype=jnp.int32)
-    step = (ns_grid[None, :] * chan_ids[:, None]) & (phase_modulus - 1)
-    tables = []
-    for rows in (coarse, fine):
-        phases = (rows[None, :, None] * step[:, None, :]) & (phase_modulus - 1)
-        tables.append(sincos(phases, phase_modulus))
-    return tables
+    )(voltages, window, twiddle, slots, ew_row, ns_row)
+
+
+def transform_table(spec_total):
+    ids = np.outer(np.arange(1, spec_total // 2 + 1), np.arange(spec_total)) % spec_total
+    turn = ids * (TWO_PI / spec_total)
+    table = np.stack([np.cos(turn), -np.sin(turn)]) / math.sqrt(spec_total)
+    return table.astype(jnp.bfloat16).astype(np.float64)
+
+
+def dedisperse_kernel(series, delays, out, freq, phase, send, recv, result, send_s, recv_s):
+    tm_size, feed_size, spec_dev, beam_dev, chan_dev = series.shape
+    spec_total = spec_dev * tm_size
+    half = spec_total // 2
+    trials = delays.shape[1]
+    trial_dev = trials // tm_size
+    table = transform_table(spec_total)
+    tm = lax.axis_index("tm")
+    feed = lax.axis_index("feed")
+
+    barrier = pltpu.get_barrier_semaphore()
+    for step in range(1, tm_size):
+        other = lax.rem(tm + step, tm_size)
+        pl.semaphore_signal(barrier, inc=1, device_id=(other, feed), device_id_type=MESH)
+
+    def to_frequency(f, _):
+        lanes = pl.ds(pl.multiple_of(f * chan_dev, chan_dev), chan_dev)
+        x = [
+            series[t // spec_dev, f, t % spec_dev].astype(jnp.float32) for t in range(spec_total)
+        ]
+        even = [x[t] + x[spec_total - t] for t in range(1, half)]
+        odd = [x[t] - x[spec_total - t] for t in range(1, half)]
+        for k in range(half):
+            re = x[0] * float(table[0, k, 0]) + x[half] * float(table[0, k, half])
+            im = None
+            for t in range(1, half):
+                re = re + even[t - 1] * float(table[0, k, t])
+                term = odd[t - 1] * float(table[1, k, t])
+                im = term if im is None else im + term
+            freq[k, :beam_dev, lanes] = re.astype(jnp.bfloat16)
+            freq[k, beam_dev:, lanes] = im.astype(jnp.bfloat16)
+        return 0
+
+    lax.fori_loop(0, feed_size, to_frequency, 0)
+
+    step_rows = 16
+
+    def make_phase(i, _):
+        rows = pl.ds(pl.multiple_of(i * step_rows, step_rows), step_rows)
+        base_re, base_im = sincos(delays[rows, :] & (spec_total - 1), spec_total)
+        re, im = base_re, base_im
+        for k in range(half):
+            phase[k, rows, :trials] = re.astype(jnp.bfloat16)
+            phase[k, rows, trials:] = im.astype(jnp.bfloat16)
+            re, im = re * base_re - im * base_im, re * base_im + im * base_re
+        return 0
+
+    lax.fori_loop(0, delays.shape[0] // step_rows, make_phase, 0)
+
+    def move(k, _):
+        mixed = jnp.dot(freq[k], phase[k], preferred_element_type=jnp.float32)
+        factor = 1.0 / math.sqrt(CHANS)
+        re = (mixed[:beam_dev, :trials] - mixed[beam_dev:, trials:]) * factor
+        im = (mixed[:beam_dev, trials:] + mixed[beam_dev:, :trials]) * factor
+        for u in range(tm_size):
+            part = slice(u * trial_dev, (u + 1) * trial_dev)
+            send[u, k] = re[:, part].astype(jnp.bfloat16)
+            send[u, half + k] = im[:, part].astype(jnp.bfloat16)
+        return 0
+
+    lax.fori_loop(0, half, move, 0)
+
+    def exchange(other, slot):
+        return pltpu.make_async_remote_copy(
+            src_ref=send.at[other],
+            dst_ref=recv.at[slot],
+            send_sem=send_s.at[other],
+            recv_sem=recv_s.at[slot],
+            device_id=(other, feed),
+            device_id_type=MESH,
+        )
+
+    pl.semaphore_wait(barrier, tm_size - 1)
+    for step in range(1, tm_size):
+        exchange(lax.rem(tm + step, tm_size), tm).start()
+    recv[tm] = send[tm]
+    for step in range(1, tm_size):
+        other = lax.rem(tm + step, tm_size)
+        exchange(other, other).wait()
+
+    def to_time(u, _):
+        rows = pl.ds(pl.multiple_of(u * beam_dev, beam_dev), beam_dev)
+        re = [recv[u, k].astype(jnp.float32) for k in range(half)]
+        im = [recv[u, half + k].astype(jnp.float32) for k in range(half)]
+        for t in range(half + 1):
+            by_re = by_im = None
+            for k in range(half):
+                weight = 1.0 if 2 * (k + 1) == spec_total else 2.0
+                term_re = re[k] * float(table[0, k, t] * weight)
+                term_im = im[k] * float(table[1, k, t] * weight)
+                by_re = term_re if by_re is None else by_re + term_re
+                by_im = term_im if by_im is None else by_im + term_im
+            result[t, rows, :] = by_re + by_im
+            if 0 < t < half:
+                result[spec_total - t, rows, :] = by_re - by_im
+        return 0
+
+    lax.fori_loop(0, tm_size, to_time, 0)
+
+    def turn(t, _):
+        out[t] = result[t].T
+        return 0
+
+    lax.fori_loop(0, spec_total, turn, 0)
+
+
+def dedisperse(series, delays):
+    tm_size, feed_size, spec_dev, beam_dev, chan_dev = series.shape
+    spec_total = spec_dev * tm_size
+    half = spec_total // 2
+    chans, trials = delays.shape
+    trial_dev = trials // tm_size
+    beams = beam_dev * tm_size
+    blocks = (tm_size, 2 * half, beam_dev, trial_dev)
+    vmem = pl.BlockSpec(memory_space=pltpu.VMEM)
+    return pl.pallas_call(
+        dedisperse_kernel,
+        out_shape=jax.ShapeDtypeStruct((spec_total, trial_dev, beams), jnp.float32),
+        in_specs=[vmem] * 2,
+        out_specs=vmem,
+        scratch_shapes=[
+            pltpu.VMEM((half, 2 * beam_dev, chans), jnp.bfloat16),
+            pltpu.VMEM((half, chans, 2 * trials), jnp.bfloat16),
+            pltpu.VMEM(blocks, jnp.bfloat16),
+            pltpu.VMEM(blocks, jnp.bfloat16),
+            pltpu.VMEM((spec_total, beams, trial_dev), jnp.float32),
+            pltpu.SemaphoreType.DMA((tm_size,)),
+            pltpu.SemaphoreType.DMA((tm_size,)),
+        ],
+        compiler_params=pltpu.CompilerParams(
+            collective_id=1, has_side_effects=True, vmem_limit_bytes=48 * 1024 * 1024
+        ),
+        name="dedisperse",
+    )(series, delays)
 
 
 def local(voltages, feed_at_grid_slot, ew_grid, ns_grid, delays):
-    spec_dev = voltages.shape[1] // NFFT
     tm_size = lax.axis_size("tm")
     feed_size = lax.axis_size("feed")
-    spec_total = spec_dev * tm_size
-    chan_dev = CHANS // feed_size
-    feeds = feed_at_grid_slot.shape[0]
-
     slots = feed_at_grid_slot.reshape(ROWS, 8).T
-    placed = jnp.arange(feeds, dtype=jnp.int32)[None, :, None] == slots[:, None, :]
-    placed = placed.astype(jnp.bfloat16)
-
-    chan_ids = lax.axis_index("feed") * chan_dev + jnp.arange(chan_dev, dtype=jnp.int32) + CHANS
-    phases = (
-        jnp.arange(4, dtype=jnp.int32)[None, None, :]
-        * ew_grid[None, :, None]
-        * chan_ids[:, None, None]
-    ) & (phase_modulus - 1)
-    ew = [part.reshape(chan_dev, -1) * 0.5 for part in sincos(phases, phase_modulus)]
-    steer = jnp.concatenate(ew, axis=1).astype(jnp.bfloat16).astype(jnp.float32)
-
-    coarse, fine = ns_rotations(ns_grid, chan_ids, 16)
-    factor = 1.0 / math.sqrt(ROWS)
-    rot = jnp.stack([coarse[0] * factor, coarse[1] * factor, fine[0], fine[1]])
-
+    ew_row = (ew_grid[:, None] * jnp.arange(4, dtype=jnp.int32)[None, :]).reshape(1, -1)
+    ns_row = ns_grid.reshape(1, -1)
     beam_dev = ew_grid.shape[0] * ns_grid.shape[0] // (tm_size * feed_size)
-    blocks = search(voltages, placed, steer, rot, tm_size, feed_size, beam_dev)
-    by_beam = blocks.transpose(0, 2, 3, 1, 4).reshape(spec_total, beam_dev, CHANS)
-
-    half = spec_total // 2
-    factor = 1.0 / math.sqrt(spec_total)
-    freq_ids = np.arange(1, half + 1)
-    turn = np.outer(freq_ids, np.arange(spec_total)) % spec_total * (TWO_PI / spec_total)
-    table = np.stack([np.cos(turn), -np.sin(turn)]) * factor
-    time_table = jnp.asarray(table.astype(jnp.bfloat16))
-    spectrum = jnp.einsum("rkt,tbc->krbc", time_table, by_beam, preferred_element_type=jnp.float32)
-    spectrum = spectrum.astype(jnp.bfloat16).reshape(half, 2 * beam_dev, CHANS)
-    base_re, base_im = sincos(delays & (spec_total - 1), spec_total)
-    powers_re, powers_im = [base_re], [base_im]
-    for _ in range(1, half):
-        re, im = powers_re[-1], powers_im[-1]
-        powers_re.append(re * base_re - im * base_im)
-        powers_im.append(re * base_im + im * base_re)
-    phase = jnp.stack([jnp.stack(powers_re), jnp.stack(powers_im)], axis=2).astype(jnp.bfloat16)
-    phase = phase.reshape(half, CHANS, -1)
-    moved = jnp.einsum("kmc,kcd->kmd", spectrum, phase, preferred_element_type=jnp.float32)
-    moved = moved.reshape(half, 2, beam_dev, 2, -1)
-    moved_real = moved[:, 0, :, 0] - moved[:, 1, :, 1]
-    moved_imag = moved[:, 0, :, 1] + moved[:, 1, :, 0]
-    folded = jnp.stack([moved_real, moved_imag]) * (1.0 / math.sqrt(CHANS))
-    folded = folded.astype(jnp.bfloat16)
-    combined = lax.all_to_all(folded, "tm", split_axis=3, concat_axis=2, tiled=True)
-    weight = np.where(2 * freq_ids == spec_total, 1.0, 2.0)[None, :, None]
-    back = jnp.asarray((table.astype(jnp.bfloat16).astype(np.float64) * weight).astype(jnp.bfloat16))
-    return jnp.einsum("rkbd,rkt->dbt", combined, back, preferred_element_type=jnp.float32)
+    series = search(voltages, slots, ew_row, ns_row, tm_size, feed_size, beam_dev)
+    return dedisperse(series, delays).transpose(1, 2, 0)
 
 
 def solution(mesh):

time: 297 us -> 177 us (0.60); the launches traced: 294 us -> 177 us
  other arithmetic: 76.3 us -> 0.72 us
  local copies, waits for them, and re-layouts: 25.1 us -> 4.88 us
  blocking collectives: 11.8 us -> 0 us
  Pallas kernels: 176 us -> 171 us
  matrix products: 3.77 us -> 0 us
    unnamed x13 -> x0, other arithmetic: 48.3 us -> none
    pallas_call x1, Pallas kernels: 176 us -> 148 us  [search(): pl.pallas_call(search_kernel, out_shape=jax.ShapeDtypeStruct(sent, jnp.bf...]
    pallas_call x0 -> x1, Pallas kernels: none -> 23.3 us  [dedisperse(): pl.pallas_call(dedisperse_kernel, out_shape=jax.ShapeDtypeStruct((spec_to...]
    another operation x4 -> x0, other arithmetic: 15 us -> none  [the longest x1 5.76 us: local(): jnp.stack(powers_re)]
    all_to_all x1 -> x0, blocking collectives: 11.8 us -> none  [local(): lax.all_to_all(folded, 'tm', split_axis=3, concat_axis=2, tiled=True)]
    convert_element_type x3 -> x0, other arithmetic: 6.34 us -> none  [the longest x1 6.21 us: local(): placed = placed.astype(jnp.bfloat16)]
    convert_element_type x4 -> x0, local copies, waits for them, and re-layouts: 5.63 us -> none  [the longest x1 2.34 us: local(): jnp.stack([jnp.stack(powers_re), jnp.stack(powers_im)], axis=2)]
    reshape x3 -> x0, local copies, waits for them, and re-layouts: 5.53 us -> none  [the longest x1 2.84 us: local(): moved = moved.reshape(half, 2, beam_dev, 2, -1)]
where the time goes in v2:
time: 177 us
  Pallas kernels  171 us (97%)
  local copies, waits for them, and re-layouts  4.88 us (3%)
    pallas_call x1, Pallas kernels, search(): pl.pallas_call(search_kernel, out_shape=jax.ShapeDtypeStruct(sent, jnp.bf...  148 us
    pallas_call x1, Pallas kernels, dedisperse(): pl.pallas_call(dedisperse_kernel, out_shape=jax.ShapeDtypeStruct((spec_to...  23.3 us

profile of v2, /device:TPU:0, one launch (start us, length us, event | category | flops | bytes accessed | tf_op | source)
XLA Modules:
  0.0 177.1 jit_solution(3976138742087857150)
XLA Ops:
  0.0 0.7 iota_multiply_fusion
  0.7 0.6 mul.26.ew_row
  1.3 0.8 reshape.30
  2.1 0.7 copy.9
  2.8 0.0 copy-start.1
  2.8 148.2 %search.1.series = bf16[4,8,4,32,128]{4,3,2,1,0:T(8,128)(2,1)} custom-call(s32[256,8192]{1,0:T(8,128)} %volt.1, f32[4,2048]{1,0:T(4,128)} %constant.4.clone.window, bf16[8,256,2048]{2,1,0:T(8,128)(2,1)} %constant.5.clone.twiddle_hbm, s32[8,256]{1,0:T(8,128)} %bitcast.4, s32[1,16]{1,0:T(1,128)} %mul.26.ew_row, s32[1,256]{1,0:T(1,128)} %bitcast.5), custom_call_target="tpu_custom_call" | custom-call | tf_op jit(solution)/shard_map/search/pallas_call | solution.py:512
  151.0 0.0 copy-done.1
  151.0 0.0 copy-start
  151.0 1.2 copy-done
  152.2 23.3 %dedisperse.1 = f32[16,128,128]{2,1,0:T(8,128)S(1)} custom-call(bf16[4,8,4,32,128]{4,3,2,1,0:T(8,128)(2,1)S(1)} %copy-done, s32[1024,512]{1,0:T(8,128)S(1)} %copy-done.1), custom_call_target="tpu_custom_call" | custom-call | tf_op jit(solution)/shard_map/dedisperse/pallas_call | solution.py:670
  175.6 1.6 copy.10
Async XLA Ops:
  2.8 148.2 %copy-start.1 = (s32[1024,512]{1,0:T(8,128)S(1)}, s32[1024,512]{1,0:T(8,128)}, u32[]{:S(2)}) copy-start(s32[1024,512]{1,0:T(8,128)} %delays.1) | copy-start | bytes 6291460
  151.0 1.2 copy-start

commit v3 on v2

--- a/solution.py
+++ b/solution.py
@@ -158,6 +158,7 @@
 
 
 MESH = pl.DeviceIdType.MESH
+REACH = 8
 
 
 def sincos(phases, modulus):
@@ -201,8 +202,8 @@
 
 def search_kernel(
     volt, window, twiddle_hbm, slots, ew_row, ns_row, out,
-    raw, frames, hist, filtered, send, spec, twiddle, placed_v, grid, east, steer, rot_v, power,
-    beams, raw_s, twiddle_s, hist_ss, hist_rs, spec_ss, spec_rs, beam_ss, beam_rs,
+    raw, frames, hist, filtered, send, spec, twiddle, placed_v, grid, east, steer, coarse, fine,
+    power, beams, raw_s, twiddle_s, hist_ss, hist_rs, spec_ss, spec_rs, beam_ss, beam_rs,
 ):
     spec_dev, feed_dev, length = frames.shape
     feed_size = spec.shape[1]
@@ -265,8 +266,6 @@
     history(TAPS - 2).start()
     for s in range(spec_dev - 2, -1, -1):
         convert(s)
-        if s >= spec_dev - TAPS + 1:
-            history(s - (spec_dev - TAPS + 1)).start()
     twiddle_copy.wait()
 
     live = jnp.where(tm > 0, 1.0, 0.0).astype(jnp.float32)
@@ -340,18 +339,19 @@
         for part, value in enumerate(turns):
             value = (value * 0.5).astype(jnp.bfloat16).astype(jnp.float32)
             steer[:, part * 4 * ews : (part + 1) * 4 * ews] = value
-        fine_rows = rot_v.shape[2]
-        row_ids = lax.broadcasted_iota(jnp.int32, (fine_rows, ns_beams), 0)
+        centres, reach = coarse.shape[2], fine.shape[2]
+        centre_ids = lax.broadcasted_iota(jnp.int32, (centres, ns_beams), 0) * (4 * reach)
+        centre_ids = centre_ids + (2 * reach - 1)
+        reach_ids = lax.broadcasted_iota(jnp.int32, (reach, ns_beams), 0) * 2 + 1
+        half_modulus = 2 * phase_modulus
         factor = 1.0 / math.sqrt(ROWS)
 
         def rotations(c, _):
-            phases = row_ids * ((ns_row[...] * (first + c)) & (phase_modulus - 1))
-            fine = sincos(phases & (phase_modulus - 1), phase_modulus)
-            coarse = sincos((phases * fine_rows) & (phase_modulus - 1), phase_modulus)
-            rot_v[0, c] = coarse[0] * factor
-            rot_v[1, c] = coarse[1] * factor
-            rot_v[2, c] = fine[0]
-            rot_v[3, c] = fine[1]
+            step = (ns_row[...] * (first + c)) & (phase_modulus - 1)
+            for ids, table, size in ((centre_ids, coarse, factor), (reach_ids, fine, 1.0)):
+                re, im = sincos((ids * step) & (half_modulus - 1), half_modulus)
+                table[0, c] = re * size
+                table[1, c] = im * size
             return 0
 
         lax.fori_loop(0, chan_dev, rotations, 0)
@@ -405,12 +405,13 @@
 
     def mix_north(count):
         def channel(c):
-            coarse_re, coarse_im, fine_re, fine_im = (rot_v[k, c] for k in range(4))
+            fine_re, fine_im = fine[0, c], fine[1, c]
             parts_re, parts_im = [], []
-            for r in range(coarse_re.shape[0]):
-                a_re, a_im = coarse_re[r : r + 1, :], coarse_im[r : r + 1, :]
-                parts_re.append((a_re * fine_re - a_im * fine_im).astype(jnp.bfloat16))
-                parts_im.append((a_re * fine_im + a_im * fine_re).astype(jnp.bfloat16))
+            for r in range(coarse.shape[2]):
+                a_re, a_im = coarse[0, c, r : r + 1, :], coarse[1, c, r : r + 1, :]
+                rr, ii, ri, ir = a_re * fine_re, a_im * fine_im, a_re * fine_im, a_im * fine_re
+                parts_re.append(jnp.concatenate([rr - ii, rr + ii], axis=0).astype(jnp.bfloat16))
+                parts_im.append(jnp.concatenate([ir + ri, ir - ri], axis=0).astype(jnp.bfloat16))
             side = east[c, : count * 2 * pairs, :].astype(jnp.bfloat16)
             by_re = jnp.dot(
                 side, jnp.concatenate(parts_re, axis=0), preferred_element_type=jnp.float32
@@ -451,9 +452,8 @@
             device_id_type=MESH,
         )
 
-    groups = [(s, s) for s in range(min(spec_dev, 2) - 1, -1, -1)]
-    if spec_dev > 2:
-        groups = [(spec_dev - 1, 2)] + groups
+    middle = spec_dev // 2
+    groups = [(spec_dev - 1, middle), (middle - 1, 0)]
 
     def form(group):
         high, low = groups[group]
@@ -468,21 +468,28 @@
         lax.fori_loop(1, tm_size * feed_size, go, 0)
         out[tm, feed, low : high + 1] = beams[tm, feed, low : high + 1]
 
-    def beamform(s):
-        for group, (high, low) in enumerate(groups):
-            if low <= s <= high:
-                arrive(s)
-                place(s)
-                mix_east(s - low)
-                if s == low:
-                    form(group)
+    def gather_east(s):
+        arrive(s)
+        place(s)
+        mix_east(s - middle if s >= middle else s)
 
     channelize(spec_dev - 1)
     make_tables()
+    waiting = TAPS - 3
     for s in range(spec_dev - 2, -1, -1):
+        if waiting >= 0:
+            history(waiting + 1).wait_send()
+            history(waiting).start()
+            waiting -= 1
         channelize(s)
-        beamform(s + 1)
-    beamform(0)
+        if s + 1 > middle:
+            gather_east(s + 1)
+        if s == middle - 1:
+            gather_east(middle)
+    form(0)
+    for s in range(middle - 1, -1, -1):
+        gather_east(s)
+    form(1)
     for group, (high, low) in enumerate(groups):
         def finish(step, _):
             peer = other_device(step)
@@ -490,8 +497,7 @@
             return 0
 
         lax.fori_loop(1, tm_size * feed_size, finish, 0)
-    for i in range(TAPS - 1):
-        history(i).wait_send()
+    history(0).wait_send()
 
 
 def search(voltages, slots, ew_row, ns_row, tm_size, feed_size, beam_dev):
@@ -500,11 +506,10 @@
     chan_dev = CHANS // feed_size
     ns_beams = ns_row.shape[1]
     pairs = 2 * ew_row.shape[1] // 4
-    fine_rows = math.isqrt(ROWS)
     window = jnp.asarray(window_constant(TAPS, NFFT))
     twiddle = jnp.asarray(dft_constant(NFFT, CHANS, feed_size))
     blocks = (spec_dev, feed_size, 2 * chan_dev, feed_dev)
-    batch = max(spec_dev - 2, 1)
+    batch = spec_dev - spec_dev // 2
     vmem = pl.BlockSpec(memory_space=pltpu.VMEM)
     hbm = pl.BlockSpec(memory_space=pl.ANY)
     dma = pltpu.SemaphoreType.DMA
@@ -526,7 +531,8 @@
             pltpu.VMEM((slots.shape[0], 2 * chan_dev, ROWS), jnp.float32),
             pltpu.VMEM((chan_dev, batch * 2 * pairs, ROWS), jnp.float32),
             pltpu.VMEM((chan_dev, 2 * ew_row.shape[1]), jnp.float32),
-            pltpu.VMEM((4, chan_dev, fine_rows, ns_beams), jnp.float32),
+            pltpu.VMEM((2, chan_dev, ROWS // (2 * REACH), ns_beams), jnp.float32),
+            pltpu.VMEM((2, chan_dev, REACH, ns_beams), jnp.float32),
             pltpu.VMEM((batch, chan_dev, pairs, ns_beams), jnp.float32),
             pltpu.VMEM(sent, jnp.bfloat16),
             dma((2,)),
@@ -535,8 +541,8 @@
             dma((TAPS - 1,)),
             dma((spec_dev, feed_size)),
             dma((spec_dev, feed_size)),
-            dma((3, tm_size, feed_size)),
-            dma((3, tm_size, feed_size)),
+            dma((2, tm_size, feed_size)),
+            dma((2, tm_size, feed_size)),
         ],
         compiler_params=pltpu.CompilerParams(
             collective_id=0, has_side_effects=True, vmem_limit_bytes=60 * 1024 * 1024
@@ -608,34 +614,37 @@
         im = (mixed[:beam_dev, trials:] + mixed[beam_dev:, :trials]) * factor
         for u in range(tm_size):
             part = slice(u * trial_dev, (u + 1) * trial_dev)
-            send[u, k] = re[:, part].astype(jnp.bfloat16)
-            send[u, half + k] = im[:, part].astype(jnp.bfloat16)
+            send[u, 2 * k] = re[:, part].astype(jnp.bfloat16)
+            send[u, 2 * k + 1] = im[:, part].astype(jnp.bfloat16)
         return 0
 
-    lax.fori_loop(0, half, move, 0)
-
-    def exchange(other, slot):
+    def exchange(part, other, slot):
+        ids = pl.ds(part * half, half)
         return pltpu.make_async_remote_copy(
-            src_ref=send.at[other],
-            dst_ref=recv.at[slot],
-            send_sem=send_s.at[other],
-            recv_sem=recv_s.at[slot],
+            src_ref=send.at[other, ids],
+            dst_ref=recv.at[slot, ids],
+            send_sem=send_s.at[part, other],
+            recv_sem=recv_s.at[part, slot],
             device_id=(other, feed),
             device_id_type=MESH,
         )
 
+    edges = (0, half // 2, half)
     pl.semaphore_wait(barrier, tm_size - 1)
-    for step in range(1, tm_size):
-        exchange(lax.rem(tm + step, tm_size), tm).start()
+    for part in range(2):
+        lax.fori_loop(edges[part], edges[part + 1], move, 0)
+        for step in range(1, tm_size):
+            exchange(part, lax.rem(tm + step, tm_size), tm).start()
     recv[tm] = send[tm]
-    for step in range(1, tm_size):
-        other = lax.rem(tm + step, tm_size)
-        exchange(other, other).wait()
+    for part in range(2):
+        for step in range(1, tm_size):
+            other = lax.rem(tm + step, tm_size)
+            exchange(part, other, other).wait()
 
     def to_time(u, _):
         rows = pl.ds(pl.multiple_of(u * beam_dev, beam_dev), beam_dev)
-        re = [recv[u, k].astype(jnp.float32) for k in range(half)]
-        im = [recv[u, half + k].astype(jnp.float32) for k in range(half)]
+        re = [recv[u, 2 * k].astype(jnp.float32) for k in range(half)]
+        im = [recv[u, 2 * k + 1].astype(jnp.float32) for k in range(half)]
         for t in range(half + 1):
             by_re = by_im = None
             for k in range(half):
@@ -678,8 +687,8 @@
             pltpu.VMEM(blocks, jnp.bfloat16),
             pltpu.VMEM(blocks, jnp.bfloat16),
             pltpu.VMEM((spec_total, beams, trial_dev), jnp.float32),
-            pltpu.SemaphoreType.DMA((tm_size,)),
-            pltpu.SemaphoreType.DMA((tm_size,)),
+            pltpu.SemaphoreType.DMA((2, tm_size)),
+            pltpu.SemaphoreType.DMA((2, tm_size)),
         ],
         compiler_params=pltpu.CompilerParams(
             collective_id=1, has_side_effects=True, vmem_limit_bytes=48 * 1024 * 1024
@@ -691,7 +700,8 @@
 def local(voltages, feed_at_grid_slot, ew_grid, ns_grid, delays):
     tm_size = lax.axis_size("tm")
     feed_size = lax.axis_size("feed")
-    slots = feed_at_grid_slot.reshape(ROWS, 8).T
+    slots = feed_at_grid_slot.reshape(-1, 2, REACH, 8)
+    slots = jnp.stack([slots[:, 1], slots[:, 0, ::-1]], axis=1).reshape(ROWS, 8).T
     ew_row = (ew_grid[:, None] * jnp.arange(4, dtype=jnp.int32)[None, :]).reshape(1, -1)
     ns_row = ns_grid.reshape(1, -1)
     beam_dev = ew_grid.shape[0] * ns_grid.shape[0] // (tm_size * feed_size)

time: 177 us -> 167 us (0.944)
  Pallas kernels: 171 us -> 161 us
    pallas_call x1, Pallas kernels: 148 us -> 141 us  [search(): pl.pallas_call(search_kernel, out_shape=jax.ShapeDtypeStruct(sent, jnp.bf...]
    pallas_call x1, Pallas kernels: 23.3 us -> 20 us  [dedisperse(): pl.pallas_call(dedisperse_kernel, out_shape=jax.ShapeDtypeStruct((spec_to...]
where the time goes in v3:
time: 167 us
  Pallas kernels  161 us (96%)
  local copies, waits for them, and re-layouts  4.95 us (3%)
    pallas_call x1, Pallas kernels, search(): pl.pallas_call(search_kernel, out_shape=jax.ShapeDtypeStruct(sent, jnp.bf...  141 us
    pallas_call x1, Pallas kernels, dedisperse(): pl.pallas_call(dedisperse_kernel, out_shape=jax.ShapeDtypeStruct((spec_to...  20 us

profile of v3, /device:TPU:0, one launch (start us, length us, event | category | flops | bytes accessed | tf_op | source)
XLA Modules:
  0.0 167.2 jit_solution(273517030663928062)
XLA Ops:
  0.0 0.7 iota_multiply_fusion
  0.7 0.7 mul.26.ew_row
  1.4 0.8 reshape.33
  2.2 0.7 copy.11
  2.9 0.0 copy-start.1
  2.9 141.5 %search.1.series = bf16[4,8,4,32,128]{4,3,2,1,0:T(8,128)(2,1)} custom-call(s32[256,8192]{1,0:T(8,128)} %volt.1, f32[4,2048]{1,0:T(4,128)} %constant.4.clone.window, bf16[8,256,2048]{2,1,0:T(8,128)(2,1)} %constant.5.clone.twiddle_hbm, s32[8,256]{1,0:T(8,128)} %bitcast.6, s32[1,16]{1,0:T(1,128)} %mul.26.ew_row, s32[1,256]{1,0:T(1,128)} %bitcast.7), custom_call_target="tpu_custom_call" | custom-call | tf_op jit(solution)/shard_map/search/pallas_call | solution.py:517
  144.4 0.0 copy-done.1
  144.4 0.0 copy-start
  144.4 1.2 copy-done
  145.6 20.0 %dedisperse.1 = f32[16,128,128]{2,1,0:T(8,128)S(1)} custom-call(bf16[4,8,4,32,128]{4,3,2,1,0:T(8,128)(2,1)S(1)} %copy-done, s32[1024,512]{1,0:T(8,128)S(1)} %copy-done.1), custom_call_target="tpu_custom_call" | custom-call | tf_op jit(solution)/shard_map/dedisperse/pallas_call | solution.py:679
  165.6 1.6 copy.10
  (3 shorter events, 0.0 us)
Async XLA Ops:
  2.9 141.5 %copy-start.1 = (s32[1024,512]{1,0:T(8,128)S(1)}, s32[1024,512]{1,0:T(8,128)}, u32[]{:S(2)}) copy-start(s32[1024,512]{1,0:T(8,128)} %delays.1) | copy-start | bytes 6291460
  144.4 1.2 copy-start

commit v4 on v3

--- a/solution.py
+++ b/solution.py
@@ -426,11 +426,11 @@
                 power[k, c] = beam_re * beam_re + beam_im * beam_im
 
         def body(i, _):
-            for c in range(4):
-                channel(i * 4 + c)
-            return 0
-
-        lax.fori_loop(0, chan_dev // 4, body, 0)
+            for c in range(8):
+                channel(i * 8 + c)
+            return 0
+
+        lax.fori_loop(0, chan_dev // 8, body, 0)
 
     def transpose_power(s, k):
         width = beam_dev * tm_size

time: 167 us -> 166 us (level)
  no operation moved by 1% of the time
where the time goes in v4:
time: 166 us
  Pallas kernels  160 us (96%)
  local copies, waits for them, and re-layouts  4.95 us (3%)
    pallas_call x1, Pallas kernels, search(): pl.pallas_call(search_kernel, out_shape=jax.ShapeDtypeStruct(sent, jnp.bf...  140 us
    pallas_call x1, Pallas kernels, dedisperse(): pl.pallas_call(dedisperse_kernel, out_shape=jax.ShapeDtypeStruct((spec_to...  20 us

profile of v4, /device:TPU:0, one launch (start us, length us, event | category | flops | bytes accessed | tf_op | source)
XLA Modules:
  0.0 165.6 jit_solution(11791407255741485877)
XLA Ops:
  0.0 0.7 iota_multiply_fusion
  0.7 0.7 mul.26.ew_row
  1.4 0.8 reshape.33
  2.2 0.7 copy.11
  2.9 0.0 copy-start.1
  2.9 139.9 %search.1.series = bf16[4,8,4,32,128]{4,3,2,1,0:T(8,128)(2,1)} custom-call(s32[256,8192]{1,0:T(8,128)} %volt.1, f32[4,2048]{1,0:T(4,128)} %constant.4.clone.window, bf16[8,256,2048]{2,1,0:T(8,128)(2,1)} %constant.5.clone.twiddle_hbm, s32[8,256]{1,0:T(8,128)} %bitcast.6, s32[1,16]{1,0:T(1,128)} %mul.26.ew_row, s32[1,256]{1,0:T(1,128)} %bitcast.7), custom_call_target="tpu_custom_call" | custom-call | tf_op jit(solution)/shard_map/search/pallas_call | solution.py:517
  142.8 0.0 copy-done.1
  142.8 0.0 copy-start
  142.8 1.2 copy-done
  144.0 20.0 %dedisperse.1 = f32[16,128,128]{2,1,0:T(8,128)S(1)} custom-call(bf16[4,8,4,32,128]{4,3,2,1,0:T(8,128)(2,1)S(1)} %copy-done, s32[1024,512]{1,0:T(8,128)S(1)} %copy-done.1), custom_call_target="tpu_custom_call" | custom-call | tf_op jit(solution)/shard_map/dedisperse/pallas_call | solution.py:679
  164.0 1.6 copy.10
  (3 shorter events, 0.0 us)
Async XLA Ops:
  2.9 139.9 %copy-start.1 = (s32[1024,512]{1,0:T(8,128)S(1)}, s32[1024,512]{1,0:T(8,128)}, u32[]{:S(2)}) copy-start(s32[1024,512]{1,0:T(8,128)} %delays.1) | copy-start | bytes 6291460
  142.8 1.2 copy-start
